TPU v7x, 32 devices: a whole 2x2x4 slice. The times are simulated.
32 devices in a mesh: gx: 8 (over z, y), gz: 4 (over x, core).
Axes of the slice: x: 2, y: 2, z: 4, core: 2. Of those that a mesh axis runs over, the one named last changes fastest.
Arguments:
- whitened: float32 [2, 64, 1024, 512], P(None, 'gz', 'gx'), may hold values from -6 to 6
- observed: float32 [2, 1024, 512], P(None, 'gx'), may hold values from -12 to 12
- lower_x: bfloat16 [1024, 1024], P('gx'), as said below
- lower_y: bfloat16 [512, 512], P('gx'), as said below
- lower_z: bfloat16 [64, 64], replicated, as said below
- coupling_kernel: float32 [2, 3, 3, 3], replicated, may hold values from -1.25 to 1.25
Outputs:
- gradient: float32 [2, 64, 1024, 512], P(None, 'gz', 'gx')
- misfit: float32 [2, 1024, 512], P(None, 'gx')
Inputs may be any that keep to these rules, and one draw needn't show every extreme that they name: `lower_x`: lower triangular: zero above the diagonal, diagonal entries between 0.5 and 1.5. `lower_y`: lower triangular: zero above the diagonal, diagonal entries between 0.5 and 1.5. `lower_z`: lower triangular: zero above the diagonal, diagonal entries between 0.5 and 1.5.
All inputs are finite; a program needn't handle non-finite values.
Results may differ from a plain program's by a relative error of at most 0.013.
The roundings to bfloat16 on the way count: a program that leaves them out, or rounds other values in their place, can miss the bound.
Values may be sent and summed in bfloat16 or wider, within the bound.
A program may use at most 128 MiB of HBM per device.

v0:
```python
import math
import jax
import jax.numpy as jnp
from jax import lax
from jax.sharding import PartitionSpec as P

NZ = 64


def padded_2(x, sides, width):
    for axis, dim in sides:
        peers, length = (lax.axis_size(axis), x.shape[dim])
        up = [(i, (i + 1) % peers) for i in range(peers - 1)]
        down = [(j, i) for i, j in up]
        last = lax.slice_in_dim(x, length - width, length, axis=dim)
        first = lax.slice_in_dim(x, 0, width, axis=dim)
        before = lax.ppermute(last, axis, up)
        after = lax.ppermute(first, axis, down)
        x = jnp.concatenate([before, x, after], axis=dim)
    return x


def depth_lines(values, local_step):
    turned = lax.all_to_all(values, "gz", split_axis=3, concat_axis=1, tiled=True)
    return lax.all_to_all(local_step(turned), "gz", split_axis=1, concat_axis=3, tiled=True)


def across_lines(values, local_step):
    turned = lax.all_to_all(values, "gx", split_axis=3, concat_axis=2, tiled=True)
    return lax.all_to_all(local_step(turned), "gx", split_axis=2, concat_axis=3, tiled=True)


def stencil_sum(padded, kernel, depth_rows, x_rows, y_rows, flipped):
    total = jnp.zeros(padded.shape[:-3] + (depth_rows, x_rows, y_rows), jnp.float32)
    for offset_z in range(3):
        for offset_x in range(3):
            for offset_y in range(3):
                start_z = 2 - offset_z if flipped else offset_z
                start_x = 2 - offset_x if flipped else offset_x
                start_y = 2 - offset_y if flipped else offset_y
                total = (
                    total
                    + kernel[offset_z, offset_x, offset_y]
                    * padded[
                        ...,
                        start_z : start_z + depth_rows,
                        start_x : start_x + x_rows,
                        start_y : start_y + y_rows,
                    ]
                )
    return total


def depth_weights(first_row, depth_rows):
    depth = (first_row + jnp.arange(depth_rows)).astype(jnp.float32)
    factor = 4.0 / math.sqrt(NZ)
    return (factor / (1.0 + depth / NZ) ** 2, factor / (1.0 + depth / NZ) ** 3)


def coupling_forward(rim, magnetic_f, kernel, shape):
    depth_rows, x_rows, y_rows = shape
    pre_scale = stencil_sum(rim, kernel[0], depth_rows, x_rows, y_rows, False)
    pre_shift = stencil_sum(rim, kernel[1], depth_rows, x_rows, y_rows, False)
    scale = jnp.tanh(pre_scale)
    growth = jnp.exp(scale)
    return (scale, growth, magnetic_f * growth + pre_shift)


def local(whitened, observed, lower_x, lower_y, lower_z, coupling_kernel):
    factor_x, factor_y = (
        lax.all_gather(lower_x, "gx", axis=0, tiled=True),
        lax.all_gather(lower_y, "gx", axis=0, tiled=True),
    )

    def apply_depth(values):
        return jnp.einsum(
            "zk,fkxy->fzxy", lower_z, values, preferred_element_type=jnp.float32
        ).astype(jnp.bfloat16)

    def apply_across(values):
        return jnp.einsum(
            "xk,fzky->fzxy", factor_x, values, preferred_element_type=jnp.float32
        ).astype(jnp.bfloat16)

    def depth_adjoint(values):
        return jnp.einsum(
            "kz,fkxy->fzxy", lower_z, values, preferred_element_type=jnp.float32
        ).astype(jnp.bfloat16)

    def across_adjoint(values):
        return jnp.einsum(
            "kx,fzky->fzxy", factor_x, values, preferred_element_type=jnp.float32
        ).astype(jnp.bfloat16)

    start = whitened.astype(jnp.bfloat16)
    first = jnp.einsum("fzxk,yk->fzxy", start, factor_y, preferred_element_type=jnp.float32).astype(
        jnp.bfloat16
    )
    model = across_lines(depth_lines(first, apply_depth), apply_across)
    density = model[0]
    magnetic_f = model[1].astype(jnp.float32)
    depth_rows, x_rows, y_rows = density.shape
    rim = padded_2(density, (("gx", 1), ("gz", 0)), 1)
    rim = jnp.pad(rim, ((0, 0), (0, 0), (1, 1))).astype(jnp.float32)
    scale, growth, coupled = coupling_forward(
        rim, magnetic_f, coupling_kernel, (depth_rows, x_rows, y_rows)
    )
    weight_g, weight_m = depth_weights(lax.axis_index("gz") * depth_rows, depth_rows)
    part_g = jnp.einsum("z,zxy->xy", weight_g, density.astype(jnp.float32))
    part_m = jnp.einsum("z,zxy->xy", weight_m, coupled)
    predicted = lax.psum(jnp.stack([part_g, part_m]), "gz")
    misfit = predicted - observed
    back_g = weight_g[:, None, None] * misfit[0][None]
    back_m = weight_m[:, None, None] * misfit[1][None]
    back_scale = (back_m * magnetic_f * growth * (1.0 - scale * scale)).astype(jnp.bfloat16)
    back_shift = back_m.astype(jnp.bfloat16)
    cotangents = jnp.stack([back_scale, back_shift])
    outer = padded_2(cotangents, (("gx", 2), ("gz", 1)), 1)
    outer = jnp.pad(outer, ((0, 0), (0, 0), (0, 0), (1, 1))).astype(jnp.float32)
    spread_back = stencil_sum(outer[0], coupling_kernel[0], depth_rows, x_rows, y_rows, True)
    spread_back = spread_back + stencil_sum(
        outer[1], coupling_kernel[1], depth_rows, x_rows, y_rows, True
    )
    adjoint = jnp.stack([back_g + spread_back, back_m * growth]).astype(jnp.bfloat16)
    fourth = depth_lines(across_lines(adjoint, across_adjoint), depth_adjoint)
    gradient = whitened + jnp.einsum(
        "fzxk,ky->fzxy", fourth, factor_y, preferred_element_type=jnp.float32
    )
    return (gradient, misfit)


def solution(mesh):
    in_specs = (
        P(None, "gz", "gx", None),
        P(None, "gx", None),
        P("gx", None),
        P("gx", None),
        P(),
        P(),
    )
    out_specs = (P(None, "gz", "gx", None), P(None, "gx", None))
    return jax.shard_map(local, mesh=mesh, in_specs=in_specs, out_specs=out_specs, check_vma=False)
```

profile of v0, /device:TPU:0, one launch (start us, length us, event | category | flops | bytes accessed | tf_op | source)
XLA Modules:
  0.0 1367.9 jit_solution(581240853023325873)
XLA Ops:
  7.2 33.2 %all_gather.6 = bf16[512,512]{1,0:T(8,128)(2,1)S(1)} all-gather(bf16[64,512]{1,0:T(8,128)(2,1)} %param.9), channel_id=1, replica_groups=mesh['gx'=8,'gz'=4] {'gx'}, dimensions={0}, use_global_device_ids=true | all-gather | bytes 589824 | tf_op jit(solution)/shard_map/all_gather | solution.py:72
  41.2 7.8 fusion.77
  49.0 7.9 copy.51
  56.9 53.9 %all_to_all.141 = bf16[2,16,128,512]{2,1,0,3:T(8,128)(2,1)} all-to-all(bf16[2,16,128,512]{2,1,0,3:T(8,128)(2,1)} %copy.51), channel_id=1, replica_groups=mesh['gx'=8,'gz'=4] {'gz'}, dimensions={3} | all-to-all | bytes 8388608 | tf_op jit(solution)/shard_map/all_to_all | solution.py:24
  110.7 9.0 copy.52
  119.7 3.4 convert_bitcast_fusion.3
  123.1 2.7 copy.53
  125.8 51.6 %all_to_all.142 = bf16[2,64,128,128]{3,2,0,1:T(8,128)(2,1)} all-to-all(bf16[2,64,128,128]{3,2,0,1:T(8,128)(2,1)S(1)} %copy.53), channel_id=1, replica_groups=mesh['gx'=8,'gz'=4] {'gz'}, dimensions={1} | all-to-all | bytes 8388608 | tf_op jit(solution)/shard_map/all_to_all | solution.py:25
  177.4 7.8 copy.95
  185.3 5.7 all-to-all-start.2
  191.7 117.5 %all-to-all-done.2 = bf16[2,16,128,512]{2,1,0,3:T(8,128)(2,1)} async-done(((bf16[2,16,128,512]{2,1,0,3:T(8,128)(2,1)}), bf16[2,16,128,512]{2,1,0,3:T(8,128)(2,1)}, u32[]{:S(2)}, u32[]{:S(2)}) %all-to-all-start.2) | async-done | bytes 4194336 | tf_op jit(solution)/shard_map/all_to_all | solution.py:29
  309.2 6.9 copy.58
  316.1 7.3 all_to_all.113
  323.4 9.5 convert_bitcast_fusion.2
  332.8 12.9 copy.59
  345.7 10.5 reshape.38
  356.2 4.7 all-to-all-start.3
  363.3 90.1 %all-to-all-done.3 = bf16[8,2,131072]{2,1,0:T(2,128)(2,1)} async-done(((bf16[8,2,131072]{2,1,0:T(2,128)(2,1)}), bf16[8,2,131072]{2,1,0:T(2,128)(2,1)}, u32[]{:S(2)}, u32[]{:S(2)}) %all-to-all-start.3) | async-done | bytes 4194336 | tf_op jit(solution)/shard_map/all_to_all | solution.py:30
  453.4 10.3 reshape.39
  463.7 9.3 copy.97
  473.0 4.8 fusion.95
  478.4 2.8 fusion.96
  481.2 2.0 copy.63
  483.2 2.0 copy.64
  486.4 4.5 collective-permute-start
  491.7 3.0 copy.89
  494.7 1.8 copy.65
  496.5 1.8 copy.66
  503.2 2.8 copy.62
  506.6 11.2 fusion.10
  517.8 122.0 %add_add_fusion = (bf16[16,128,512]{1,2,0:T(8,128)(2,1)S(1)}, f32[16,128,512]{1,2,0:T(8,128)}) fusion(f32[16,128,512]{1,2,0:T(8,128)} %bitcast.166, f32[18,130,514]{1,2,0:T(8,128)} %fusion.10, f32[]{:T(128)} %bitcast.79, f32[]{:T(128)} %bitcast.78, f32[]{:T(128)} %bitcast.77, f32[]{:T(128)} %bitcast.76, f32[]{:T(128)} %bitcast.75, f32[]{:T(128)} %bitcast.74, ...), kind=kLoop, calls=%fused_computation.148 | loop fusion | flops 114294784 | bytes 123732184 | tf_op jit(solution)/shard_map/add | solution.py:66
  639.8 3.0 copy.91
  642.8 2.0 fusion.90
  645.7 35.0 %all-reduce.4.cloned.1.call-done = f32[2,128,512]{2,1,0:T(8,128)} async-done(((f32[2,128,512]{2,1,0:T(8,128)}), f32[2,128,512]{2,1,0:T(8,128)}) %all-reduce.4.cloned.1.call-update) | async-done | bytes 524304 | tf_op jit(solution)/shard_map/psum | solution.py:111
  683.3 6.4 fusion.81
  689.7 4.5 slice_maximum_fusion
  694.2 3.6 copy.70
  697.9 3.4 collective-permute-start.4
  701.3 4.0 copy.71
  706.6 3.2 copy.72
  711.1 3.2 copy.73
  714.3 2.9 pad_maximum_fusion.5
  720.2 3.2 collective-permute-done.7
  723.4 22.6 %fusion.1 = f32[2,18,130,514]{2,3,1,0:T(8,128)S(1)} fusion(bf16[2,1,130,512]{2,3,1,0:T(8,128)(2,1)} %collective-permute-done.7, bf16[2,1,130,512]{2,3,1,0:T(8,128)(2,1)S(1)} %collective-permute-done.6, bf16[2,16,1,512]{2,3,1,0:T(8,128)(2,1)} %copy.73, bf16[2,16,1,512]{2,3,1,0:T(8,128)(2,1)} %copy.72, bf16[1,16,128,512]{2,3,1,0:T(8,128)(2,1)S(1)} %multiply_convert_fusion, ...), kind=kLoop, calls=%fused_computation.8 | loop fusion | flops 50515920 | bytes 14414400 | tf_op jit(solution)/shard_map/convert_element_type | solution.py:119
  746.0 6.9 slice_bitcast_fusion.1
  752.9 196.9 %fusion.84 = bf16[1,16,128,512]{2,3,1,0:T(8,128)(2,1)S(1)} fusion(f32[18,130,514]{1,2,0:T(8,128)} %get-tuple-element.5, f32[]{:T(128)} %bitcast.79, f32[]{:T(128)} %bitcast.78, f32[]{:T(128)} %bitcast.77, f32[]{:T(128)} %bitcast.76, f32[]{:T(128)} %bitcast.75, f32[]{:T(128)} %bitcast.74, f32[]{:T(128)} %bitcast.73, f32[]{:T(128)} %bitcast.72, f32[]{:T(128)} %bitcast.71, ...), kind=kLoop, calls=%fused_computation.161 | loop fusion | flops 115343360 | bytes 228852000 | tf_op jit(solution)/shard_map/stack | solution.py:124
  950.2 2.7 copy.74
  952.9 97.5 %all_to_all.143 = bf16[2,16,128,512]{2,1,0,3:T(8,128)(2,1)S(1)} all-to-all(bf16[2,16,128,512]{2,1,0,3:T(8,128)(2,1)S(1)} %copy.74), channel_id=1, replica_groups=mesh['gx'=8,'gz'=4] {'gx'}, dimensions={3} | all-to-all | bytes 8388608 | tf_op jit(solution)/shard_map/all_to_all | solution.py:29
  1050.4 4.7 copy.76
  1055.1 7.4 all_to_all.120
  1062.6 8.4 convert_bitcast_fusion.1
  1071.0 12.9 copy.77
  1083.9 10.5 reshape.40
  1094.3 97.9 %all_to_all.144 = bf16[8,2,131072]{2,1,0:T(2,128)(2,1)} all-to-all(bf16[8,2,131072]{2,1,0:T(2,128)(2,1)} %reshape.40), channel_id=1, replica_groups=mesh['gx'=8,'gz'=4] {'gx'}, dimensions={0} | all-to-all | bytes 8388608 | tf_op jit(solution)/shard_map/all_to_all | solution.py:30
  1192.2 10.3 reshape.41
  1202.5 14.8 %copy.101 = bf16[2,16,128,8,64]{2,1,0,4,3:T(8,128)(2,1)} copy(bf16[2,16,128,8,64]{4,1,0,2,3:T(8,128)(2,1)} %bitcast.171) | data formatting | bytes 8388608 | tf_op jit(solution)/shard_map/all_to_all | solution.py:30
  1217.2 54.1 %all_to_all.145 = bf16[2,16,128,512]{2,1,0,3:T(8,128)(2,1)} all-to-all(bf16[2,16,128,512]{2,1,0,3:T(8,128)(2,1)} %bitcast.173), channel_id=1, replica_groups=mesh['gx'=8,'gz'=4] {'gz'}, dimensions={3} | all-to-all | bytes 8388608 | tf_op jit(solution)/shard_map/all_to_all | solution.py:24
  1271.3 9.0 copy.82
  1280.3 3.5 convert_bitcast_fusion
  1283.8 2.7 copy.84
  1286.5 50.7 %all_to_all.146 = bf16[2,64,128,128]{3,2,0,1:T(8,128)(2,1)S(1)} all-to-all(bf16[2,64,128,128]{3,2,0,1:T(8,128)(2,1)S(1)} %copy.84), channel_id=1, replica_groups=mesh['gx'=8,'gz'=4] {'gz'}, dimensions={1} | all-to-all | bytes 8388608 | tf_op jit(solution)/shard_map/all_to_all | solution.py:25
  1337.2 5.9 copy.109
  1343.2 7.2 all_to_all.132
  1350.4 10.4 convolution_add_fusion
  (63 shorter events, 21.2 us)
Async XLA Ops:
  7.2 112.5 %copy-start = (bf16[64,64]{1,0:T(8,128)(2,1)S(1)}, bf16[64,64]{1,0:T(8,128)(2,1)}, u32[]{:S(2)}) copy-start(bf16[64,64]{1,0:T(8,128)(2,1)} %param.10) | copy-start | bytes 24580
  40.4 0.8 copy-start.7
  185.3 123.9 %all-to-all-start.2 = ((bf16[2,16,128,512]{2,1,0,3:T(8,128)(2,1)}), bf16[2,16,128,512]{2,1,0,3:T(8,128)(2,1)}, u32[]{:S(2)}, u32[]{:S(2)}) async-start(bf16[2,16,128,512]{2,1,0,3:T(8,128)(2,1)} %bitcast.174), calls=%async_computation.2 | async-start | bytes 8388608 | tf_op jit(solution)/shard_map/all_to_all | solution.py:29
  191.0 132.4 %all-gather.2.cloned.1.call-start = ((), (), s32[]{:S(2)}) async-start(), calls=%async_computation.8 | async-start | bytes 2359296 | tf_op jit(solution)/shard_map/all_gather | solution.py:71
  356.2 4.9 copy-start.11
  356.2 97.2 %all-to-all-start.3 = ((bf16[8,2,131072]{2,1,0:T(2,128)(2,1)}), bf16[8,2,131072]{2,1,0:T(2,128)(2,1)}, u32[]{:S(2)}, u32[]{:S(2)}) async-start(bf16[8,2,131072]{2,1,0:T(2,128)(2,1)} %reshape.38), calls=%async_computation.3 | async-start | bytes 8388608 | tf_op jit(solution)/shard_map/all_to_all | solution.py:30
  360.9 319.8 %all-reduce.4.cloned.1.call-start = ((), (), s32[]{:S(2)}) async-start(), calls=%async_computation.9 | async-start | bytes 1048576 | tf_op jit(solution)/shard_map/psum | solution.py:111
  485.1 11.4 collective-permute-start.1
  486.4 8.3 collective-permute-start
  498.3 4.3 copy-start.5
  498.3 4.8 copy-start.4
  499.9 6.0 collective-permute-start.2
  501.4 4.6 collective-permute-start.3
  503.1 2.8 copy-start.2
  503.2 3.4 copy-start.3
  639.8 41.0 %copy-start.10 = (f32[2,128,512]{2,1,0:T(8,128)S(1)}, f32[2,128,512]{2,1,0:T(8,128)}, u32[]{:S(2)}) copy-start(f32[2,128,512]{2,1,0:T(8,128)} %param.7) | copy-start | bytes 1572868
  681.9 0.8 copy-start.9
  689.7 4.5 copy-start.1
  697.9 8.7 collective-permute-start.4
  705.3 5.8 collective-permute-start.5
  717.2 3.0 collective-permute-start.6
  718.5 4.9 collective-permute-start.7
  752.9 196.9 %copy-start.6 = (bf16[1,16,128,512]{2,3,1,0:T(8,128)(2,1)S(1)}, bf16[1,16,128,512]{2,3,1,0:T(8,128)(2,1)}, u32[]{:S(2)}) copy-start(bf16[1,16,128,512]{2,3,1,0:T(8,128)(2,1)} %get-tuple-element.11) | copy-start | bytes 6291460
  1055.1 7.4 copy-start.12
  1343.1 7.3 copy-start.8
Sparse Core Ops, SparseCore 0:
  193.9 102.6 all-gather.1
  645.8 34.8 all-reduce.3
where the time goes:
time: 1380 us; the launch traced here: 1370 us
  blocking collectives  439 us (32%)
  other arithmetic  376 us (27%)
  waiting for transfers between devices  248 us (18%)
  local copies, waits for them, and re-layouts  219 us (16%)
  matrix products  45.4 us (3%)
  starting transfers between devices  26.9 us (2%)
  between operations  14.6 us (1%)
    another operation x2, other arithmetic, local(): jnp.stack([back_g + spread_back, back_m * growth]).astype(jnp.bfloat16)  197 us
    add x1, other arithmetic, coupling_forward(): return (scale, growth, magnetic_f * growth + pre_shift)  122 us
    all_to_all x1, waiting for transfers between devices, across_lines(): lax.all_to_all(values, 'gx', split_axis=3, concat_axis=2, tiled=True)  117 us
    all_to_all x2, blocking collectives, depth_lines(): lax.all_to_all(values, 'gz', split_axis=3, concat_axis=1, tiled=True)  108 us
    all_to_all x2, blocking collectives, depth_lines(): lax.all_to_all(local_step(turned), 'gz', split_axis=1, concat_axis=3, til...  102 us
    all_to_all x1, blocking collectives, across_lines(): lax.all_to_all(local_step(turned), 'gx', split_axis=2, concat_axis=3, til...  97.9 us
    all_to_all x1, blocking collectives, across_lines(): lax.all_to_all(values, 'gx', split_axis=3, concat_axis=2, tiled=True)  97.5 us
    all_to_all x1, waiting for transfers between devices, across_lines(): lax.all_to_all(local_step(turned), 'gx', split_axis=2, concat_axis=3, til...  90.1 us
  transfers between devices with their start and end apart: 12, of which 6 were waited for; matrix products, arithmetic and copies ran while one was open for 2% of the time, Pallas kernels for 0%

commit v1 on v0

--- a/solution.py
+++ b/solution.py
@@ -108,7 +108,9 @@
     weight_g, weight_m = depth_weights(lax.axis_index("gz") * depth_rows, depth_rows)
     part_g = jnp.einsum("z,zxy->xy", weight_g, density.astype(jnp.float32))
     part_m = jnp.einsum("z,zxy->xy", weight_m, coupled)
-    predicted = lax.psum(jnp.stack([part_g, part_m]), "gz")
+    own = jnp.stack([part_g, part_m])
+    parts = lax.all_gather(own, "gz", axis=0, tiled=False)
+    predicted = parts.sum(axis=0)
     misfit = predicted - observed
     back_g = weight_g[:, None, None] * misfit[0][None]
     back_m = weight_m[:, None, None] * misfit[1][None]

time: 1380 us -> 1370 us (level)
    psum x1 -> x0, waiting for transfers between devices: 35 us -> none  [local(): predicted = lax.psum(jnp.stack([part_g, part_m]), 'gz')]
    all_gather x0 -> x1, waiting for transfers between devices: none -> 24.5 us  [local(): parts = lax.all_gather(own, 'gz', axis=0, tiled=False)]
where the time goes in v1:
time: 1370 us; the launch traced here: 1360 us
  blocking collectives  439 us (32%)
  other arithmetic  377 us (28%)
  waiting for transfers between devices  237 us (17%)
  local copies, waits for them, and re-layouts  218 us (16%)
  matrix products  45.4 us (3%)
  starting transfers between devices  27.3 us (2%)
  between operations  14.6 us (1%)
    another operation x2, other arithmetic, local(): jnp.stack([back_g + spread_back, back_m * growth]).astype(jnp.bfloat16)  197 us
    add x1, other arithmetic, coupling_forward(): return (scale, growth, magnetic_f * growth + pre_shift)  122 us
    all_to_all x1, waiting for transfers between devices, across_lines(): lax.all_to_all(values, 'gx', split_axis=3, concat_axis=2, tiled=True)  117 us
    all_to_all x2, blocking collectives, depth_lines(): lax.all_to_all(values, 'gz', split_axis=3, concat_axis=1, tiled=True)  108 us
    all_to_all x2, blocking collectives, depth_lines(): lax.all_to_all(local_step(turned), 'gz', split_axis=1, concat_axis=3, til...  102 us
    all_to_all x1, blocking collectives, across_lines(): lax.all_to_all(local_step(turned), 'gx', split_axis=2, concat_axis=3, til...  97.9 us
    all_to_all x1, blocking collectives, across_lines(): lax.all_to_all(values, 'gx', split_axis=3, concat_axis=2, tiled=True)  97.5 us
    all_to_all x1, waiting for transfers between devices, across_lines(): lax.all_to_all(local_step(turned), 'gx', split_axis=2, concat_axis=3, til...  90.1 us
  transfers between devices with their start and end apart: 12, of which 6 were waited for; matrix products, arithmetic and copies ran while one was open for 2% of the time, Pallas kernels for 0%

profile of v1, /device:TPU:0, one launch (start us, length us, event | category | flops | bytes accessed | tf_op | source)
XLA Modules:
  0.0 1358.2 jit_solution(16255518293962539466)
XLA Ops:
  7.2 33.2 %all_gather.12 = bf16[512,512]{1,0:T(8,128)(2,1)S(1)} all-gather(bf16[64,512]{1,0:T(8,128)(2,1)} %param.9), channel_id=1, replica_groups=mesh['gx'=8,'gz'=4] {'gx'}, dimensions={0}, use_global_device_ids=true | all-gather | bytes 589824 | tf_op jit(solution)/shard_map/all_gather | solution.py:72
  41.2 7.8 fusion.77
  49.0 7.9 copy.51
  56.9 53.9 %all_to_all.141 = bf16[2,16,128,512]{2,1,0,3:T(8,128)(2,1)} all-to-all(bf16[2,16,128,512]{2,1,0,3:T(8,128)(2,1)} %copy.51), channel_id=1, replica_groups=mesh['gx'=8,'gz'=4] {'gz'}, dimensions={3} | all-to-all | bytes 8388608 | tf_op jit(solution)/shard_map/all_to_all | solution.py:24
  110.7 9.0 copy.52
  119.7 3.4 convert_bitcast_fusion.3
  123.1 2.7 copy.53
  125.8 51.6 %all_to_all.142 = bf16[2,64,128,128]{3,2,0,1:T(8,128)(2,1)} all-to-all(bf16[2,64,128,128]{3,2,0,1:T(8,128)(2,1)S(1)} %copy.53), channel_id=1, replica_groups=mesh['gx'=8,'gz'=4] {'gz'}, dimensions={1} | all-to-all | bytes 8388608 | tf_op jit(solution)/shard_map/all_to_all | solution.py:25
  177.4 7.8 copy.95
  185.3 5.7 all-to-all-start.2
  191.7 117.5 %all-to-all-done.2 = bf16[2,16,128,512]{2,1,0,3:T(8,128)(2,1)} async-done(((bf16[2,16,128,512]{2,1,0,3:T(8,128)(2,1)}), bf16[2,16,128,512]{2,1,0,3:T(8,128)(2,1)}, u32[]{:S(2)}, u32[]{:S(2)}) %all-to-all-start.2) | async-done | bytes 4194336 | tf_op jit(solution)/shard_map/all_to_all | solution.py:29
  309.2 6.9 copy.58
  316.1 7.3 all_to_all.113
  323.4 9.5 convert_bitcast_fusion.2
  332.8 12.9 copy.59
  345.7 10.5 reshape.39
  356.2 4.7 all-to-all-start.3
  363.3 90.1 %all-to-all-done.3 = bf16[8,2,131072]{2,1,0:T(2,128)(2,1)} async-done(((bf16[8,2,131072]{2,1,0:T(2,128)(2,1)}), bf16[8,2,131072]{2,1,0:T(2,128)(2,1)}, u32[]{:S(2)}, u32[]{:S(2)}) %all-to-all-start.3) | async-done | bytes 4194336 | tf_op jit(solution)/shard_map/all_to_all | solution.py:30
  453.4 10.3 reshape.40
  463.7 9.3 copy.97
  473.0 4.8 fusion.95
  478.4 2.8 fusion.96
  481.2 2.0 copy.63
  483.2 2.0 copy.64
  486.4 4.5 collective-permute-start
  491.7 3.0 copy.89
  496.5 1.8 copy.66
  503.2 2.8 copy.62
  506.6 11.2 fusion.10
  517.8 122.0 %add_add_fusion = (bf16[16,128,512]{1,2,0:T(8,128)(2,1)S(1)}, f32[16,128,512]{1,2,0:T(8,128)}) fusion(f32[16,128,512]{1,2,0:T(8,128)} %bitcast.167, f32[18,130,514]{1,2,0:T(8,128)} %fusion.10, f32[]{:T(128)} %bitcast.79, f32[]{:T(128)} %bitcast.78, f32[]{:T(128)} %bitcast.77, f32[]{:T(128)} %bitcast.76, f32[]{:T(128)} %bitcast.75, f32[]{:T(128)} %bitcast.74, ...), kind=kLoop, calls=%fused_computation.148 | loop fusion | flops 114294784 | bytes 123732184 | tf_op jit(solution)/shard_map/add | solution.py:66
  639.8 3.0 copy.91
  642.8 2.1 fusion.90
  645.8 24.5 %all-gather.6.cloned.1.call-done = f32[8,128,512]{2,1,0:T(8,128)} async-done(((f32[2,128,512]{2,1,0:T(8,128)}), f32[8,128,512]{2,1,0:T(8,128)}) %all-gather.6.cloned.1.call-update) | async-done | bytes 2097168 | tf_op jit(solution)/shard_map/all_gather | solution.py:112
  670.2 1.9 reduce_sum.9
  673.6 6.4 fusion.81
  680.0 4.5 slice_maximum_fusion
  684.5 3.6 copy.70
  688.2 3.8 collective-permute-start.4
  692.0 3.6 copy.71
  696.9 3.2 copy.72
  701.4 3.2 copy.73
  704.6 2.9 pad_maximum_fusion.5
  710.5 3.2 collective-permute-done.7
  713.7 22.6 %fusion.1 = f32[2,18,130,514]{2,3,1,0:T(8,128)S(1)} fusion(bf16[2,1,130,512]{2,3,1,0:T(8,128)(2,1)} %collective-permute-done.7, bf16[2,1,130,512]{2,3,1,0:T(8,128)(2,1)S(1)} %collective-permute-done.6, bf16[2,16,1,512]{2,3,1,0:T(8,128)(2,1)} %copy.73, bf16[2,16,1,512]{2,3,1,0:T(8,128)(2,1)} %copy.72, bf16[1,16,128,512]{2,3,1,0:T(8,128)(2,1)S(1)} %multiply_convert_fusion, ...), kind=kLoop, calls=%fused_computation.8 | loop fusion | flops 50515920 | bytes 14414400 | tf_op jit(solution)/shard_map/convert_element_type | solution.py:121
  736.4 6.9 slice_bitcast_fusion.1
  743.3 196.9 %fusion.84 = bf16[1,16,128,512]{2,3,1,0:T(8,128)(2,1)S(1)} fusion(f32[18,130,514]{1,2,0:T(8,128)} %get-tuple-element.5, f32[]{:T(128)} %bitcast.79, f32[]{:T(128)} %bitcast.78, f32[]{:T(128)} %bitcast.77, f32[]{:T(128)} %bitcast.76, f32[]{:T(128)} %bitcast.75, f32[]{:T(128)} %bitcast.74, f32[]{:T(128)} %bitcast.73, f32[]{:T(128)} %bitcast.72, f32[]{:T(128)} %bitcast.71, ...), kind=kLoop, calls=%fused_computation.161 | loop fusion | flops 115343360 | bytes 228852000 | tf_op jit(solution)/shard_map/stack | solution.py:126
  940.6 2.7 copy.74
  943.3 97.5 %all_to_all.143 = bf16[2,16,128,512]{2,1,0,3:T(8,128)(2,1)S(1)} all-to-all(bf16[2,16,128,512]{2,1,0,3:T(8,128)(2,1)S(1)} %copy.74), channel_id=1, replica_groups=mesh['gx'=8,'gz'=4] {'gx'}, dimensions={3} | all-to-all | bytes 8388608 | tf_op jit(solution)/shard_map/all_to_all | solution.py:29
  1040.8 4.7 copy.76
  1045.5 7.4 all_to_all.120
  1052.9 8.4 convert_bitcast_fusion.1
  1061.3 12.9 copy.77
  1074.2 10.5 reshape.41
  1084.7 97.9 %all_to_all.144 = bf16[8,2,131072]{2,1,0:T(2,128)(2,1)} all-to-all(bf16[8,2,131072]{2,1,0:T(2,128)(2,1)} %reshape.41), channel_id=1, replica_groups=mesh['gx'=8,'gz'=4] {'gx'}, dimensions={0} | all-to-all | bytes 8388608 | tf_op jit(solution)/shard_map/all_to_all | solution.py:30
  1182.5 10.3 reshape.42
  1192.8 14.8 %copy.101 = bf16[2,16,128,8,64]{2,1,0,4,3:T(8,128)(2,1)} copy(bf16[2,16,128,8,64]{4,1,0,2,3:T(8,128)(2,1)} %bitcast.172) | data formatting | bytes 8388608 | tf_op jit(solution)/shard_map/all_to_all | solution.py:30
  1207.6 54.1 %all_to_all.145 = bf16[2,16,128,512]{2,1,0,3:T(8,128)(2,1)} all-to-all(bf16[2,16,128,512]{2,1,0,3:T(8,128)(2,1)} %bitcast.174), channel_id=1, replica_groups=mesh['gx'=8,'gz'=4] {'gz'}, dimensions={3} | all-to-all | bytes 8388608 | tf_op jit(solution)/shard_map/all_to_all | solution.py:24
  1261.7 9.0 copy.82
  1270.6 3.5 convert_bitcast_fusion
  1274.1 2.7 copy.84
  1276.8 50.7 %all_to_all.146 = bf16[2,64,128,128]{3,2,0,1:T(8,128)(2,1)S(1)} all-to-all(bf16[2,64,128,128]{3,2,0,1:T(8,128)(2,1)S(1)} %copy.84), channel_id=1, replica_groups=mesh['gx'=8,'gz'=4] {'gz'}, dimensions={1} | all-to-all | bytes 8388608 | tf_op jit(solution)/shard_map/all_to_all | solution.py:25
  1327.6 5.9 copy.109
  1333.5 7.2 all_to_all.132
  1340.8 10.4 convolution_add_fusion
  (64 shorter events, 22.0 us)
Async XLA Ops:
  7.2 112.5 %copy-start = (bf16[64,64]{1,0:T(8,128)(2,1)S(1)}, bf16[64,64]{1,0:T(8,128)(2,1)}, u32[]{:S(2)}) copy-start(bf16[64,64]{1,0:T(8,128)(2,1)} %param.10) | copy-start | bytes 24580
  40.4 0.8 copy-start.7
  185.3 123.9 %all-to-all-start.2 = ((bf16[2,16,128,512]{2,1,0,3:T(8,128)(2,1)}), bf16[2,16,128,512]{2,1,0,3:T(8,128)(2,1)}, u32[]{:S(2)}, u32[]{:S(2)}) async-start(bf16[2,16,128,512]{2,1,0,3:T(8,128)(2,1)} %bitcast.175), calls=%async_computation.2 | async-start | bytes 8388608 | tf_op jit(solution)/shard_map/all_to_all | solution.py:29
  191.0 132.4 %all-gather.4.cloned.1.call-start = ((), (), s32[]{:S(2)}) async-start(), calls=%async_computation.8 | async-start | bytes 2359296 | tf_op jit(solution)/shard_map/all_gather | solution.py:71
  356.2 4.9 copy-start.11
  356.2 97.2 %all-to-all-start.3 = ((bf16[8,2,131072]{2,1,0:T(2,128)(2,1)}), bf16[8,2,131072]{2,1,0:T(2,128)(2,1)}, u32[]{:S(2)}, u32[]{:S(2)}) async-start(bf16[8,2,131072]{2,1,0:T(2,128)(2,1)} %reshape.39), calls=%async_computation.3 | async-start | bytes 8388608 | tf_op jit(solution)/shard_map/all_to_all | solution.py:30
  360.9 309.3 %all-gather.6.cloned.1.call-start = ((), (), s32[]{:S(2)}) async-start(), calls=%async_computation.9 | async-start | bytes 2621440 | tf_op jit(solution)/shard_map/all_gather | solution.py:112
  485.1 11.4 collective-permute-start.1
  486.4 8.3 collective-permute-start
  498.3 4.3 copy-start.5
  498.3 4.8 copy-start.4
  499.9 6.0 collective-permute-start.2
  501.4 4.6 collective-permute-start.3
  503.1 2.8 copy-start.2
  503.2 3.4 copy-start.3
  642.8 29.3 %copy-start.10 = (f32[2,128,512]{2,1,0:T(8,128)S(1)}, f32[2,128,512]{2,1,0:T(8,128)}, u32[]{:S(2)}) copy-start(f32[2,128,512]{2,1,0:T(8,128)} %param.7) | copy-start | bytes 1572868
  672.2 0.8 copy-start.9
  680.0 4.5 copy-start.1
  688.2 8.7 collective-permute-start.4
  695.6 5.8 collective-permute-start.5
  707.5 3.0 collective-permute-start.6
  708.8 4.9 collective-permute-start.7
  743.3 196.9 %copy-start.6 = (bf16[1,16,128,512]{2,3,1,0:T(8,128)(2,1)S(1)}, bf16[1,16,128,512]{2,3,1,0:T(8,128)(2,1)}, u32[]{:S(2)}) copy-start(bf16[1,16,128,512]{2,3,1,0:T(8,128)(2,1)} %get-tuple-element.11) | copy-start | bytes 6291460
  1045.5 7.4 copy-start.12
  1333.5 7.3 copy-start.8
Sparse Core Ops, SparseCore 0:
  193.9 102.6 all-gather.3
  645.9 24.3 all-gather.5
